TPU v7x, 32 devices: a whole 2x2x4 slice. The times are simulated.
32 devices in a mesh: dom: 32 (over z, y, x, core).
Axes of the slice: x: 2, y: 2, z: 4, core: 2. Of those that a mesh axis runs over, the one named last changes fastest.
Arguments:
- embeddings: float32 [16384, 400], P('dom'), may hold values from -1.8 to 1.8
- row_state: float32 [16384], P('dom'), may hold values from 0.01 to 1
- relations: float32 [2048, 400], P('dom'), may hold values from 0.5 to 1.5
- relation_state: float32 [2048], P('dom'), may hold values from 0.01 to 1
- partner_mask: int32 [1], replicated, may hold values from 1 to 31
- source_rows: int32 [98304], P('dom'), may hold values from 0 to 511
- relation_ids: int32 [98304], P('dom'), may hold values from 0 to 2047
- dest_rows: int32 [98304], P('dom'), may hold values from 0 to 511
- negative_rows: int32 [384, 512], P('dom'), may hold values from 0 to 511
- edge_count: int32 [32], P('dom'), may hold values from 1 to 3072, 61440 in all
Outputs:
- new_embeddings: float32 [16384, 400], P('dom')
- new_row_state: float32 [16384], P('dom')
- new_relations: float32 [2048, 400], P('dom')
- new_relation_state: float32 [2048], P('dom')
Inputs may be any that keep to these rules, and one draw needn't show every extreme that they name: Device i trains the bucket of partition i with partition i XOR partner_mask[0]. `edge_count`: some bucket has all 3072 slots live.
All inputs are finite; a program needn't handle non-finite values. No bound on the sum of `edge_count` on one device may be relied on, other than what follows from the above.
Results may differ from a plain program's by a relative error of at most 0.0015.
Values may be sent and summed in bfloat16 or wider, within the bound.
A program may use at most 128 MiB of HBM per device.

v0:
```python
import functools

import jax
import jax.numpy as jnp
from jax import lax
from jax.experimental import pallas as pl
from jax.experimental.pallas import tpu as pltpu
from jax.sharding import PartitionSpec as P

BF = jnp.bfloat16
F32 = jnp.float32


def nn(a, b):
    return lax.dot_general(a, b, (((1,), (0,)), ((), ())), preferred_element_type=F32)


def nt(a, b):
    return lax.dot_general(a, b, (((1,), (1,)), ((), ())), preferred_element_type=F32)


def one_hot(rows, ids, first=0):
    at = lax.broadcasted_iota(jnp.int32, (rows, ids.shape[1]), 0) + first
    return at == ids


def as_bf(mask):
    return jnp.where(mask, 1.0, 0.0).astype(BF)


def sigmoid(x):
    return 0.5 * jnp.tanh(0.5 * x) + 0.5


def bucket_kernel(
    count_ref,
    own_ref,
    part_ref,
    rel_ref,
    source_ref,
    ids_ref,
    dest_ref,
    negs_ref,
    own_grad_ref,
    part_grad_ref,
    rel_grad_ref,
    own_t,
    part_t,
    rel_t,
    y_t,
    part_acc,
):
    groups, _, group_len = source_ref.shape
    negs_per = negs_ref.shape[2]
    rows, width = own_ref.shape
    rels = rel_ref.shape[0]
    eye = as_bf(
        lax.broadcasted_iota(jnp.int32, (width, width), 0)
        == lax.broadcasted_iota(jnp.int32, (width, width), 1)
    )
    own_t[...] = nt(eye, own_ref[...].astype(BF)).astype(BF)
    part_t[...] = nt(eye, part_ref[...]).astype(BF)
    rel_t[...] = nt(eye, rel_ref[...]).astype(BF)
    own_grad_ref[...] = jnp.zeros_like(own_grad_ref)
    part_acc[...] = jnp.zeros_like(part_acc)
    count = count_ref[0]

    def group(g, carry):
        from_source = as_bf(one_hot(rows, source_ref[g]))
        own_rows = nn(own_t[...], from_source)
        rel_rows = nn(rel_t[...], as_bf(one_hot(rels, ids_ref[g])))
        queries = (own_rows * rel_rows).astype(BF)
        scores = nn(part_ref[...], queries)
        to_dest = one_hot(rows, dest_ref[g])
        positive = jnp.sum(jnp.where(to_dest, scores, 0.0), axis=0, keepdims=True)
        edge = lax.broadcasted_iota(jnp.int32, (1, group_len), 1) + g * group_len
        live = jnp.where(edge < count, 1.0, 0.0)
        pos_grad = -live * sigmoid(-positive)
        times = jnp.sum(
            jnp.where(one_hot(rows, negs_ref[g]), 1.0 / negs_per, 0.0), axis=1, keepdims=True
        )
        weight = times * (live * sigmoid(scores)) + jnp.where(to_dest, pos_grad, 0.0)
        high = weight.astype(BF)
        low = jnp.where(to_dest, weight - high.astype(F32), 0.0).astype(BF)
        query_grad = nn(part_t[...], high) + nn(part_t[...], low)
        part_acc[...] += nt(high, queries) + nt(low, queries)
        own_grad_ref[...] += nt(from_source, (query_grad * rel_rows).astype(BF))
        columns = pl.ds(pl.multiple_of(g * group_len, group_len), group_len)
        y_t[:, columns] = (query_grad * own_rows).astype(BF)
        return carry

    lax.fori_loop(0, groups, group, 0)
    part_grad_ref[...] = part_acc[...].astype(BF)

    chunk = min(rels, rows)

    def scatter(c, carry):
        first = pl.multiple_of(c * chunk, chunk)
        total = jnp.zeros((chunk, width), F32)
        for g in range(groups):
            hot = as_bf(one_hot(chunk, ids_ref[g], first))
            total = total + nt(hot, y_t[:, g * group_len : (g + 1) * group_len])
        rel_grad_ref[pl.ds(first, chunk), :] = total
        return carry

    lax.fori_loop(0, rels // chunk, scatter, 0)


def train_bucket(embeddings, part_bf, rel_bf, source, rel_ids, dest, negatives, count):
    groups, negs_per = negatives.shape
    edges = source.shape[0]
    rows, width = embeddings.shape
    rels = rel_bf.shape[0]
    split = (groups, 1, edges // groups)
    vmem = pl.BlockSpec(memory_space=pltpu.VMEM)
    unit = 2 * edges * rows * width
    return pl.pallas_call(
        bucket_kernel,
        out_shape=(
            jax.ShapeDtypeStruct((rows, width), F32),
            jax.ShapeDtypeStruct((rows, width), BF),
            jax.ShapeDtypeStruct((rels, width), F32),
        ),
        in_specs=[pl.BlockSpec(memory_space=pltpu.SMEM)] + [vmem] * 7,
        out_specs=(vmem,) * 3,
        scratch_shapes=[
            pltpu.VMEM((width, rows), BF),
            pltpu.VMEM((width, rows), BF),
            pltpu.VMEM((width, rels), BF),
            pltpu.VMEM((width, edges), BF),
            pltpu.VMEM((rows, width), F32),
        ],
        compiler_params=pltpu.CompilerParams(vmem_limit_bytes=50 * 2**20),
        cost_estimate=pl.CostEstimate(
            flops=7 * unit + 2 * unit * rels // rows,
            bytes_accessed=8 * (rows + rels) * width,
            transcendentals=edges * rows,
        ),
        name="bucket",
    )(
        count,
        embeddings,
        part_bf,
        rel_bf,
        source.reshape(split),
        rel_ids.reshape(split),
        dest.reshape(split),
        negatives.reshape(groups, 1, negs_per),
    )


def exchange(value, mask, axis):
    size = lax.axis_size(axis)

    def with_mask(m):
        pairs = [(i, i ^ m) for i in range(size)]
        return lambda v: lax.ppermute(v, axis, pairs)

    return lax.switch(mask - 1, [with_mask(m) for m in range(1, size)], value)


def adagrad(value, state, grad):
    new_state = state + jnp.mean(grad * grad, axis=1)
    return value - 0.1 * grad / jnp.sqrt(new_state)[:, None], new_state


def local(
    embeddings,
    row_state,
    relations,
    relation_state,
    partner_mask,
    source_rows,
    relation_ids,
    dest_rows,
    negative_rows,
    edge_count,
):
    mask = partner_mask[0]
    rel_bf = lax.all_gather(relations.astype(BF), "dom", axis=0, tiled=True)
    part_bf = exchange(embeddings.astype(BF), mask, "dom")
    own_grad, part_grad, rel_grad = train_bucket(
        embeddings, part_bf, rel_bf, source_rows, relation_ids, dest_rows, negative_rows, edge_count
    )
    rel_share = lax.psum_scatter(rel_grad, "dom", scatter_dimension=0, tiled=True)
    returned = exchange(part_grad, mask, "dom")
    new_embeddings, new_row_state = adagrad(
        embeddings, row_state, own_grad + returned.astype(F32)
    )
    new_relations, new_relation_state = adagrad(relations, relation_state, rel_share)
    return (new_embeddings, new_row_state, new_relations, new_relation_state)


def solution(mesh):
    in_specs = (
        P("dom", None),
        P("dom"),
        P("dom", None),
        P("dom"),
        P(),
        P("dom"),
        P("dom"),
        P("dom"),
        P("dom", None),
        P("dom"),
    )
    out_specs = (P("dom", None), P("dom"), P("dom", None), P("dom"))
    return jax.shard_map(local, mesh=mesh, in_specs=in_specs, out_specs=out_specs, check_vma=False)
```

profile of v0, /device:TPU:0, one launch (start us, length us, event | category | flops | bytes accessed | tf_op | source)
XLA Modules:
  0.0 263.5 jit_solution(6816575737271925562)
XLA Ops:
  7.2 0.0 all-gather.2.cloned.1.call-start
  7.2 1.5 convert_element_type.167
  8.8 0.0 all-gather.2.cloned.1.call-update
  8.8 0.0 reduce-scatter.2.cloned.1.call-start
  8.8 1.2 convert_element_type.166
  10.0 1.5 copy.50.own_ref
  12.8 0.8 reshape.30.negs_ref
  13.6 0.0 copy-start
  13.6 0.0 copy-start.1
  13.6 0.0 copy-start.2
  13.6 15.8 %conditional.5 = (bf16[512,400]{1,0:T(8,128)(2,1)}) conditional(s32[]{:T(128)} %bitcast, bf16[512,400]{0,1:T(8,128)(2,1)S(1)} %convert_element_type.166, bf16[512,400]{0,1:T(8,128)(2,1)S(1)} %convert_element_type.166, bf16[512,400]{0,1:T(8,128)(2,1)S(1)} %convert_element_type.166, ...), branch_computations={%region_0.0_spmd, %region_1.0_spmd, %region_2.0_spmd, %region_3.0_... | conditional | bytes 2457648 | solution.py:159
  13.7 0.2 copy.19
  13.9 3.0 %collective-permute-start.1 = (bf16[512,400]{1,0:T(8,128)(2,1)S(1)}, bf16[512,400]{1,0:T(8,128)(2,1)}, u32[]{:S(2)}, u32[]{:S(2)}) collective-permute-start(bf16[512,400]{1,0:T(8,128)(2,1)S(1)} %copy.19), channel_id=1, source_target_pairs={{0,2},{1,3},{2,0},{3,1},{4,6},{5,7},{6,4},{7,5},{8,10},{9,11},{10,... | collective-permute-start | bytes 1228808 | tf_op jit(solution)/shard_map/cond/branch_1_fun/ppermute | solution.py:157
  16.9 12.5 %collective-permute-done.1 = bf16[512,400]{1,0:T(8,128)(2,1)} collective-permute-done((bf16[512,400]{1,0:T(8,128)(2,1)S(1)}, bf16[512,400]{1,0:T(8,128)(2,1)}, u32[]{:S(2)}, u32[]{:S(2)}) %collective-permute-start.1) | collective-permute-done | bytes 409632 | tf_op jit(solution)/shard_map/cond/branch_1_fun/ppermute | solution.py:157
  29.4 41.2 %all-gather.2.cloned.1.call-done.rel_ref = bf16[2048,400]{1,0:T(8,128)(2,1)} async-done(((bf16[64,400]{1,0:T(8,128)(2,1)}), bf16[2048,400]{1,0:T(8,128)(2,1)}) %all-gather.2.cloned.1.call-update) | async-done | bytes 1638416 | tf_op jit(solution)/shard_map/all_gather | solution.py:180
  70.6 0.0 copy-done.2
  70.6 42.9 %bucket.1 = (f32[512,400]{1,0:T(8,128)S(1)}, bf16[512,400]{1,0:T(8,128)(2,1)S(1)}, f32[2048,400]{1,0:T(8,128)}) custom-call(s32[1]{0:T(128)S(6)} %copy.115.count_ref, f32[512,400]{1,0:T(8,128)S(1)} %copy.50.own_ref, bf16[512,400]{1,0:T(8,128)(2,1)} %get-tuple-element.154.part_ref, bf16[2048,400]{1,0:T(8,128)(2,1)} %all-gather.2.cloned.1.call-done.rel_ref, ...), custom_call_target="tpu_custom_call" | custom-call | flops 18874368000 | bytes 8192000 | tf_op jit(solution)/shard_map/bucket/pallas_call | solution.py:117
  113.5 0.0 reduce-scatter.2.cloned.1.call-update
  113.5 0.0 copy-start.5
  113.5 0.0 copy-start.3
  113.6 19.4 %conditional.6 = (bf16[512,400]{1,0:T(8,128)(2,1)}) conditional(s32[]{:T(128)} %bitcast, bf16[512,400]{1,0:T(8,128)(2,1)S(1)} %get-tuple-element.140, bf16[512,400]{1,0:T(8,128)(2,1)S(1)} %get-tuple-element.140, bf16[512,400]{1,0:T(8,128)(2,1)S(1)} %get-tuple-element.140, ...), branch_computations={%region_31.0_spmd, %region_32.0_spmd, %region_33.0_spmd, %region_3... | conditional | bytes 1638448
  113.6 1.5 collective-permute-start.32
  115.1 17.9 %collective-permute-done.32 = bf16[512,400]{1,0:T(8,128)(2,1)} collective-permute-done((bf16[512,400]{1,0:T(8,128)(2,1)S(1)}, bf16[512,400]{1,0:T(8,128)(2,1)}, u32[]{:S(2)}, u32[]{:S(2)}) %collective-permute-start.32) | collective-permute-done | bytes 409632 | tf_op jit(solution)/shard_map/cond/branch_1_fun/ppermute | solution.py:157
  133.0 1.3 multiply_reduce_fusion
  134.2 0.0 copy-done.4
  134.2 0.6 fusion.1
  134.8 1.3 divide_subtract_fusion
  136.1 1.2 copy.51
  137.3 116.2 %reduce-scatter.2.cloned.1.call-done = f32[64,400]{1,0:T(8,128)} async-done(((f32[2048,400]{1,0:T(8,128)}), f32[64,400]{1,0:T(8,128)}) %reduce-scatter.2.cloned.1.call-update) | async-done | bytes 102416 | tf_op jit(solution)/shard_map/reduce_scatter | solution.py:185
  253.5 1.0 multiply_reduce_fusion.1
  254.5 0.5 fusion
  255.1 1.6 divide_subtract_fusion.1
  (5 shorter events, 0.0 us)
Async XLA Ops:
  7.2 63.5 %all-gather.2.cloned.1.call-start = ((), (), s32[]{:S(2)}) async-start(), calls=%async_computation.1 | async-start | bytes 2162688 | tf_op jit(solution)/shard_map/all_gather | solution.py:180
  8.8 244.7 %reduce-scatter.2.cloned.1.call-start = ((), (), s32[]{:S(2)}) async-start(), calls=%async_computation.2 | async-start | bytes 4325376 | tf_op jit(solution)/shard_map/reduce_scatter | solution.py:185
  13.6 57.0 %copy-start = (s32[3072]{0:T(1024)S(1)}, s32[3072]{0:T(1024)}, u32[]{:S(2)}) copy-start(s32[3072]{0:T(1024)} %param.77) | copy-start | bytes 36868
  13.6 57.0 %copy-start.1 = (s32[3072]{0:T(1024)S(1)}, s32[3072]{0:T(1024)}, u32[]{:S(2)}) copy-start(s32[3072]{0:T(1024)} %param.78) | copy-start | bytes 36868
  13.6 57.0 %copy-start.2 = (s32[3072]{0:T(1024)S(1)}, s32[3072]{0:T(1024)}, u32[]{:S(2)}) copy-start(s32[3072]{0:T(1024)} %param.79) | copy-start | bytes 36868
  13.9 15.5 %collective-permute-start.1 = (bf16[512,400]{1,0:T(8,128)(2,1)S(1)}, bf16[512,400]{1,0:T(8,128)(2,1)}, u32[]{:S(2)}, u32[]{:S(2)}) collective-permute-start(bf16[512,400]{1,0:T(8,128)(2,1)S(1)} %copy.19), channel_id=1, source_target_pairs={{0,2},{1,3},{2,0},{3,1},{4,6},{5,7},{6,4},{7,5},{8,10},{9,11},{10,... | collective-permute-start | bytes 1228808 | tf_op jit(solution)/shard_map/cond/branch_1_fun/ppermute | solution.py:157
  113.5 20.7 %copy-start.4 = (f32[512]{0:T(512)S(1)}, f32[512]{0:T(512)}, u32[]{:S(2)}) copy-start(f32[512]{0:T(512)} %param.73) | copy-start | bytes 6148
  113.5 141.0 %copy-start.5 = (f32[64]{0:T(128)S(1)}, f32[64]{0:T(128)}, u32[]{:S(2)}) copy-start(f32[64]{0:T(128)} %param.75) | copy-start | bytes 772
  113.5 141.5 %copy-start.3 = (f32[64,400]{1,0:T(8,128)S(1)}, f32[64,400]{1,0:T(8,128)}, u32[]{:S(2)}) copy-start(f32[64,400]{1,0:T(8,128)} %param.74) | copy-start | bytes 307204
  113.6 19.4 %collective-permute-start.32 = (bf16[512,400]{1,0:T(8,128)(2,1)S(1)}, bf16[512,400]{1,0:T(8,128)(2,1)}, u32[]{:S(2)}, u32[]{:S(2)}) collective-permute-start(bf16[512,400]{1,0:T(8,128)(2,1)S(1)} %param.32), channel_id=1, source_target_pairs={{0,2},{1,3},{2,0},{3,1},{4,6},{5,7},{6,4},{7,5},{8,10},{9,11},{10,... | collective-permute-start | bytes 1228808 | tf_op jit(solution)/shard_map/cond/branch_1_fun/ppermute | solution.py:157
Sparse Core Ops, SparseCore 0:
  11.4 59.1 all-gather.1
  113.6 139.8 reduce-scatter.1
where the time goes:
time: 265 us; the launch traced here: 264 us
  waiting for transfers between devices  188 us (71%)
  Pallas kernels  42.9 us (16%)
  between operations  15.4 us (6%)
  other arithmetic  9.07 us (3%)
  starting transfers between devices  4.56 us (2%)
  local copies, waits for them, and re-layouts  3.69 us (1%)
    reduce_scatter x1, waiting for transfers between devices, local(): lax.psum_scatter(rel_grad, 'dom', scatter_dimension=0, tiled=True)  116 us
    pallas_call x1, Pallas kernels, train_bucket(): pl.pallas_call(bucket_kernel, out_shape=(jax.ShapeDtypeStruct((rows, widt...  42.9 us
    all_gather x1, waiting for transfers between devices, local(): rel_bf = lax.all_gather(relations.astype(BF), 'dom', axis=0, tiled=True)  41.2 us
    ppermute x2, waiting for transfers between devices, with_mask(): return lambda v: lax.ppermute(v, axis, pairs)  30.4 us
  transfers between devices with their start and end apart: 4, of which 4 were waited for; matrix products, arithmetic and copies ran while one was open for 3% of the time, Pallas kernels for 0%

commit v1 on v0

--- a/solution.py
+++ b/solution.py
@@ -149,6 +149,120 @@
     )
 
 
+def flip(me, bit):
+    return me + bit * (1 - 2 * ((me // bit) % 2))
+
+
+def bit_order(me, bits):
+    order = [2**t for t in range(bits)]
+    if bits > 2:
+        core = me % 2
+        order[1], order[2] = 2 + 2 * core, 4 - 2 * core
+    return order
+
+
+def slot_of(device, bits):
+    slot = device * 0
+    for bit in bit_order(device, bits):
+        slot = 2 * slot + (device // bit) % 2
+    return slot
+
+
+def greet(me, bits):
+    barrier = pltpu.get_barrier_semaphore()
+    for t in range(bits):
+        pl.semaphore_signal(
+            barrier, inc=1, device_id=(flip(me, 2**t),), device_id_type=pl.DeviceIdType.MESH
+        )
+    pl.semaphore_wait(barrier, bits)
+
+
+def gather_kernel(bits, shard_ref, out_ref, send_sem, recv_sem):
+    me = lax.axis_index("dom")
+    slot = slot_of(me, bits)
+    order = bit_order(me, bits)
+    out_ref[slot] = shard_ref[...]
+    greet(me, bits)
+    for step in range(bits):
+        held = 2**step
+        blocks = out_ref.at[pl.ds((slot // held) * held, held)]
+        copy = pltpu.make_async_remote_copy(
+            src_ref=blocks,
+            dst_ref=blocks,
+            send_sem=send_sem.at[step],
+            recv_sem=recv_sem.at[step],
+            device_id=(flip(me, order[bits - 1 - step]),),
+            device_id_type=pl.DeviceIdType.MESH,
+        )
+        copy.start()
+        copy.wait()
+
+
+def gather_relations(shard, size):
+    bits = size.bit_length() - 1
+    vmem = pl.BlockSpec(memory_space=pltpu.VMEM)
+    return pl.pallas_call(
+        functools.partial(gather_kernel, bits),
+        out_shape=jax.ShapeDtypeStruct((size,) + shard.shape, shard.dtype),
+        in_specs=[vmem],
+        out_specs=vmem,
+        scratch_shapes=[pltpu.SemaphoreType.DMA((bits,)), pltpu.SemaphoreType.DMA((bits,))],
+        compiler_params=pltpu.CompilerParams(
+            collective_id=0, has_side_effects=True, vmem_limit_bytes=32 * 2**20
+        ),
+        name="gather_relations",
+    )(shard)
+
+
+def sum_kernel(bits, grad_ref, out_ref, acc, outgoing, incoming, send_sem, recv_sem):
+    me = lax.axis_index("dom")
+    order = bit_order(me, bits)
+    greet(me, bits)
+    source, first = grad_ref, 0
+    for step in range(bits):
+        half = 2 ** (bits - 1 - step)
+        at = 2**bits - 2 * half
+        mine = (me // order[step]) % 2
+        region = pl.ds(at, half)
+        outgoing[region] = source[pl.ds(first + (1 - mine) * half, half)].astype(BF)
+        copy = pltpu.make_async_remote_copy(
+            src_ref=outgoing.at[region],
+            dst_ref=incoming.at[region],
+            send_sem=send_sem.at[step],
+            recv_sem=recv_sem.at[step],
+            device_id=(flip(me, order[step]),),
+            device_id_type=pl.DeviceIdType.MESH,
+        )
+        copy.start()
+        copy.wait()
+        acc[region] = source[pl.ds(first + mine * half, half)] + incoming[region].astype(F32)
+        source, first = acc, at
+    out_ref[...] = acc[2**bits - 2]
+
+
+def sum_relations(grad, size):
+    bits = size.bit_length() - 1
+    shard = grad.shape[1:]
+    vmem = pl.BlockSpec(memory_space=pltpu.VMEM)
+    return pl.pallas_call(
+        functools.partial(sum_kernel, bits),
+        out_shape=jax.ShapeDtypeStruct(shard, F32),
+        in_specs=[vmem],
+        out_specs=vmem,
+        scratch_shapes=[
+            pltpu.VMEM(grad.shape, F32),
+            pltpu.VMEM(grad.shape, BF),
+            pltpu.VMEM(grad.shape, BF),
+            pltpu.SemaphoreType.DMA((bits,)),
+            pltpu.SemaphoreType.DMA((bits,)),
+        ],
+        compiler_params=pltpu.CompilerParams(
+            collective_id=1, has_side_effects=True, vmem_limit_bytes=50 * 2**20
+        ),
+        name="sum_relations",
+    )(grad)
+
+
 def exchange(value, mask, axis):
     size = lax.axis_size(axis)
 
@@ -177,12 +291,15 @@
     edge_count,
 ):
     mask = partner_mask[0]
-    rel_bf = lax.all_gather(relations.astype(BF), "dom", axis=0, tiled=True)
+    size = lax.axis_size("dom")
+    share, width = relations.shape
+    rel_bf = gather_relations(relations.astype(BF), size).reshape(size * share, width)
+    slots = slot_of(relation_ids // share, size.bit_length() - 1) * share + relation_ids % share
     part_bf = exchange(embeddings.astype(BF), mask, "dom")
     own_grad, part_grad, rel_grad = train_bucket(
-        embeddings, part_bf, rel_bf, source_rows, relation_ids, dest_rows, negative_rows, edge_count
-    )
-    rel_share = lax.psum_scatter(rel_grad, "dom", scatter_dimension=0, tiled=True)
+        embeddings, part_bf, rel_bf, source_rows, slots, dest_rows, negative_rows, edge_count
+    )
+    rel_share = sum_relations(rel_grad.reshape(size, share, width), size)
     returned = exchange(part_grad, mask, "dom")
     new_embeddings, new_row_state = adagrad(
         embeddings, row_state, own_grad + returned.astype(F32)

time: 265 us -> 169 us (0.64)
  waiting for transfers between devices: 188 us -> 48.8 us
  Pallas kernels: 42.9 us -> 99.3 us
  between operations: 15.4 us -> 2.02 us
    reduce_scatter x1 -> x0, waiting for transfers between devices: 116 us -> none  [local(): lax.psum_scatter(rel_grad, 'dom', scatter_dimension=0, tiled=True)]
    pallas_call x0 -> x2, Pallas kernels: none -> 56.5 us  [the longest x1 28.4 us: sum_relations(): pl.pallas_call(functools.partial(sum_kernel, bits), out_shape=jax.ShapeDt...]
    all_gather x1 -> x0, waiting for transfers between devices: 41.2 us -> none  [local(): rel_bf = lax.all_gather(relations.astype(BF), 'dom', axis=0, tiled=True)]
    ppermute x2, waiting for transfers between devices: 30.4 us -> 48.8 us  [with_mask(): return lambda v: lax.ppermute(v, axis, pairs)]
  transfers between devices with their start and end apart: 4 -> 2, of which waited for: 4 -> 2; matrix products, arithmetic and copies ran while one was open for 3% -> 0% of each run, Pallas kernels for 0% -> 0%
where the time goes in v1:
time: 169 us
  Pallas kernels  99.3 us (59%)
  waiting for transfers between devices  48.8 us (29%)
  other arithmetic  7.63 us (5%)
  starting transfers between devices  6.87 us (4%)
  local copies, waits for them, and re-layouts  3.9 us (2%)
  between operations  2.02 us (1%)
    ppermute x2, waiting for transfers between devices, with_mask(): return lambda v: lax.ppermute(v, axis, pairs)  48.8 us
    pallas_call x1, Pallas kernels, train_bucket(): pl.pallas_call(bucket_kernel, out_shape=(jax.ShapeDtypeStruct((rows, widt...  42.8 us
    pallas_call x1, Pallas kernels, sum_relations(): pl.pallas_call(functools.partial(sum_kernel, bits), out_shape=jax.ShapeDt...  28.4 us
    pallas_call x1, Pallas kernels, gather_relations(): pl.pallas_call(functools.partial(gather_kernel, bits), out_shape=jax.Shap...  28.2 us
    ppermute x2, starting transfers between devices, with_mask(): return lambda v: lax.ppermute(v, axis, pairs)  6.87 us
  transfers between devices with their start and end apart: 2, of which 2 were waited for; matrix products, arithmetic and copies ran while one was open for 0% of the time, Pallas kernels for 0%

profile of v1, /device:TPU:0, one launch (start us, length us, event | category | flops | bytes accessed | tf_op | source)
XLA Modules:
  0.0 168.6 jit_solution(9204600154951294298)
XLA Ops:
  1.9 1.0 fusion.10
  3.0 0.8 reshape.37.negs_ref
  3.8 0.9 convert_element_type.167.shard_ref
  4.7 1.2 convert_element_type.166
  5.9 0.0 copy-start.3
  5.9 0.0 copy-start.1
  5.9 0.0 copy-start.2
  5.9 28.6 %conditional.5 = (bf16[512,400]{1,0:T(8,128)(2,1)}) conditional(s32[]{:T(128)} %bitcast, bf16[512,400]{0,1:T(8,128)(2,1)S(1)} %convert_element_type.166, bf16[512,400]{0,1:T(8,128)(2,1)S(1)} %convert_element_type.166, bf16[512,400]{0,1:T(8,128)(2,1)S(1)} %convert_element_type.166, ...), branch_computations={%region_0.1_spmd, %region_1.2_spmd, %region_2.3_spmd, %region_3.4_... | conditional | bytes 2457648 | solution.py:273
  6.0 0.2 copy.37
  6.2 5.1 %collective-permute-start.19 = (bf16[512,400]{1,0:T(8,128)(2,1)S(1)}, bf16[512,400]{1,0:T(8,128)(2,1)}, u32[]{:S(2)}, u32[]{:S(2)}) collective-permute-start(bf16[512,400]{1,0:T(8,128)(2,1)S(1)} %copy.37), channel_id=1, source_target_pairs={{0,20},{1,21},{2,22},{3,23},{4,16},{5,17},{6,18},{7,19},{8,28},{9,... | collective-permute-start | bytes 1228808 | tf_op jit(solution)/shard_map/cond/branch_19_fun/ppermute | solution.py:271
  11.2 23.3 %collective-permute-done.19 = bf16[512,400]{1,0:T(8,128)(2,1)} collective-permute-done((bf16[512,400]{1,0:T(8,128)(2,1)S(1)}, bf16[512,400]{1,0:T(8,128)(2,1)}, u32[]{:S(2)}, u32[]{:S(2)}) %collective-permute-start.19) | collective-permute-done | bytes 409632 | tf_op jit(solution)/shard_map/cond/branch_19_fun/ppermute | solution.py:271
  34.5 0.0 copy-done.3
  34.5 0.3 copy.50.own_ref
  34.8 28.2 %gather_relations.1 = bf16[32,64,400]{2,1,0:T(8,128)(2,1)S(1)} custom-call(bf16[64,400]{1,0:T(8,128)(2,1)S(1)} %convert_element_type.167.shard_ref), custom_call_target="tpu_custom_call" | custom-call | tf_op jit(solution)/shard_map/gather_relations/pallas_call | solution.py:204
  63.0 0.0 copy-start
  63.0 1.4 copy-done
  64.4 0.0 copy-done.1
  64.4 0.0 copy-done.2
  64.4 42.8 %bucket.1 = (f32[512,400]{1,0:T(8,128)S(1)}, bf16[512,400]{1,0:T(8,128)(2,1)S(1)}, f32[2048,400]{1,0:T(8,128)}) custom-call(s32[1]{0:T(128)S(6)} %copy.115.count_ref, f32[512,400]{1,0:T(8,128)S(1)} %copy.50.own_ref, bf16[512,400]{1,0:T(8,128)(2,1)} %get-tuple-element.154.part_ref, bf16[2048,400]{1,0:T(8,128)(2,1)} %bitcast.6, s32[12,1,256]{2,1,0:T(1,128)S(1)} %bitcast.8, ...), custom_call_target="tpu_custom_call" | custom-call | flops 18874368000 | bytes 8192000 | tf_op jit(solution)/shard_map/bucket/pallas_call | solution.py:117
  107.2 27.4 %conditional.6 = (bf16[512,400]{1,0:T(8,128)(2,1)}) conditional(s32[]{:T(128)} %bitcast, bf16[512,400]{1,0:T(8,128)(2,1)S(1)} %get-tuple-element.140, bf16[512,400]{1,0:T(8,128)(2,1)S(1)} %get-tuple-element.140, bf16[512,400]{1,0:T(8,128)(2,1)S(1)} %get-tuple-element.140, ...), branch_computations={%region_31.32_spmd, %region_32.33_spmd, %region_33.34_spmd, %regio... | conditional | bytes 1638448
  107.2 1.8 %collective-permute-start.50 = (bf16[512,400]{1,0:T(8,128)(2,1)S(1)}, bf16[512,400]{1,0:T(8,128)(2,1)}, u32[]{:S(2)}, u32[]{:S(2)}) collective-permute-start(bf16[512,400]{1,0:T(8,128)(2,1)S(1)} %param.50), channel_id=1, source_target_pairs={{0,20},{1,21},{2,22},{3,23},{4,16},{5,17},{6,18},{7,19},{8,28},{9,... | collective-permute-start | bytes 1228808 | tf_op jit(solution)/shard_map/cond/branch_19_fun/ppermute | solution.py:271
  109.0 25.6 %collective-permute-done.50 = bf16[512,400]{1,0:T(8,128)(2,1)} collective-permute-done((bf16[512,400]{1,0:T(8,128)(2,1)S(1)}, bf16[512,400]{1,0:T(8,128)(2,1)}, u32[]{:S(2)}, u32[]{:S(2)}) %collective-permute-start.50) | collective-permute-done | bytes 409632 | tf_op jit(solution)/shard_map/cond/branch_19_fun/ppermute | solution.py:271
  134.6 28.4 %sum_relations.1 = f32[64,400]{1,0:T(8,128)S(1)} custom-call(f32[32,64,400]{2,1,0:T(8,128)} %bitcast.10), custom_call_target="tpu_custom_call" | custom-call | tf_op jit(solution)/shard_map/sum_relations/pallas_call | solution.py:247
  162.9 0.1 multiply_reduce_fusion.1
  163.0 0.0 copy-done.6
  163.0 0.5 fusion.22
  163.6 0.0 copy-done.4
  163.6 0.7 divide_subtract_fusion.1
  164.3 1.3 multiply_reduce_fusion
  165.6 0.6 fusion.23
  166.2 1.3 divide_subtract_fusion
  167.4 1.2 copy.51
  (4 shorter events, 0.0 us)
Async XLA Ops:
  5.9 28.6 %copy-start.3 = (f32[512,400]{0,1:T(8,128)S(1)}, f32[512,400]{0,1:T(8,128)}, u32[]{:S(2)}) copy-start(f32[512,400]{0,1:T(8,128)} %param.72) | copy-start | bytes 2457604
  5.9 58.5 %copy-start.1 = (s32[3072]{0:T(1024)S(1)}, s32[3072]{0:T(1024)}, u32[]{:S(2)}) copy-start(s32[3072]{0:T(1024)} %param.77) | copy-start | bytes 36868
  5.9 58.5 %copy-start.2 = (s32[3072]{0:T(1024)S(1)}, s32[3072]{0:T(1024)}, u32[]{:S(2)}) copy-start(s32[3072]{0:T(1024)} %param.79) | copy-start | bytes 36868
  6.2 28.3 %collective-permute-start.19 = (bf16[512,400]{1,0:T(8,128)(2,1)S(1)}, bf16[512,400]{1,0:T(8,128)(2,1)}, u32[]{:S(2)}, u32[]{:S(2)}) collective-permute-start(bf16[512,400]{1,0:T(8,128)(2,1)S(1)} %copy.37), channel_id=1, source_target_pairs={{0,20},{1,21},{2,22},{3,23},{4,16},{5,17},{6,18},{7,19},{8,28},{9,... | collective-permute-start | bytes 1228808 | tf_op jit(solution)/shard_map/cond/branch_19_fun/ppermute | solution.py:271
  63.0 1.4 copy-start
  107.2 55.9 %copy-start.6 = (f32[64]{0:T(128)S(1)}, f32[64]{0:T(128)}, u32[]{:S(2)}) copy-start(f32[64]{0:T(128)} %param.75) | copy-start | bytes 772
  107.2 56.4 %copy-start.4 = (f32[64,400]{1,0:T(8,128)S(1)}, f32[64,400]{1,0:T(8,128)}, u32[]{:S(2)}) copy-start(f32[64,400]{1,0:T(8,128)} %param.74) | copy-start | bytes 307204
  107.2 58.4 %copy-start.5 = (f32[512]{0:T(512)S(1)}, f32[512]{0:T(512)}, u32[]{:S(2)}) copy-start(f32[512]{0:T(512)} %param.73) | copy-start | bytes 6148
  107.2 27.4 %collective-permute-start.50 = (bf16[512,400]{1,0:T(8,128)(2,1)S(1)}, bf16[512,400]{1,0:T(8,128)(2,1)}, u32[]{:S(2)}, u32[]{:S(2)}) collective-permute-start(bf16[512,400]{1,0:T(8,128)(2,1)S(1)} %param.50), channel_id=1, source_target_pairs={{0,20},{1,21},{2,22},{3,23},{4,16},{5,17},{6,18},{7,19},{8,28},{9,... | collective-permute-start | bytes 1228808 | tf_op jit(solution)/shard_map/cond/branch_19_fun/ppermute | solution.py:271

commit v2 on v1

--- a/solution.py
+++ b/solution.py
@@ -210,6 +210,9 @@
         compiler_params=pltpu.CompilerParams(
             collective_id=0, has_side_effects=True, vmem_limit_bytes=32 * 2**20
         ),
+        cost_estimate=pl.CostEstimate(
+            flops=0, bytes_accessed=64 * size * shard.size, transcendentals=0
+        ),
         name="gather_relations",
     )(shard)
 
@@ -259,18 +262,21 @@
         compiler_params=pltpu.CompilerParams(
             collective_id=1, has_side_effects=True, vmem_limit_bytes=50 * 2**20
         ),
+        cost_estimate=pl.CostEstimate(
+            flops=0, bytes_accessed=64 * grad.size, transcendentals=0
+        ),
         name="sum_relations",
     )(grad)
 
 
-def exchange(value, mask, axis):
+def exchange(value, mask, axis, beside, operand):
     size = lax.axis_size(axis)
 
     def with_mask(m):
         pairs = [(i, i ^ m) for i in range(size)]
-        return lambda v: lax.ppermute(v, axis, pairs)
-
-    return lax.switch(mask - 1, [with_mask(m) for m in range(1, size)], value)
+        return lambda v, x: (lax.ppermute(v, axis, pairs), beside(x, size))
+
+    return lax.switch(mask - 1, [with_mask(m) for m in range(1, size)], value, operand)
 
 
 def adagrad(value, state, grad):
@@ -293,14 +299,17 @@
     mask = partner_mask[0]
     size = lax.axis_size("dom")
     share, width = relations.shape
-    rel_bf = gather_relations(relations.astype(BF), size).reshape(size * share, width)
     slots = slot_of(relation_ids // share, size.bit_length() - 1) * share + relation_ids % share
-    part_bf = exchange(embeddings.astype(BF), mask, "dom")
+    part_bf, rel_bf = exchange(
+        embeddings.astype(BF), mask, "dom", gather_relations, relations.astype(BF)
+    )
+    rel_bf = rel_bf.reshape(size * share, width)
     own_grad, part_grad, rel_grad = train_bucket(
         embeddings, part_bf, rel_bf, source_rows, slots, dest_rows, negative_rows, edge_count
     )
-    rel_share = sum_relations(rel_grad.reshape(size, share, width), size)
-    returned = exchange(part_grad, mask, "dom")
+    returned, rel_share = exchange(
+        part_grad, mask, "dom", sum_relations, rel_grad.reshape(size, share, width)
+    )
     new_embeddings, new_row_state = adagrad(
         embeddings, row_state, own_grad + returned.astype(F32)
     )

time: 169 us -> 151 us (0.89); the launches traced: 169 us -> 153 us
  waiting for transfers between devices: 48.8 us -> 0.01 us
  loops' own time: 0.06 us -> 15.9 us
  Pallas kernels: 99.3 us -> 114 us
    ppermute x2, waiting for transfers between devices: 48.8 us -> 0.01 us  [with_mask(): return lambda v, x: (lax.ppermute(v, axis, pairs), beside(x, size))]
    pallas_call x1, Pallas kernels: 28.2 us -> 45.1 us  [gather_relations(): pl.pallas_call(functools.partial(gather_kernel, bits), out_shape=jax.Shap...]
    unnamed x1, loops' own time: 0.01 us -> 15.2 us
    pallas_call x1, Pallas kernels: 42.8 us -> 40.8 us  [train_bucket(): pl.pallas_call(bucket_kernel, out_shape=(jax.ShapeDtypeStruct((rows, widt...]
    unnamed x16 -> x14, local copies, waits for them, and re-layouts: 2.92 us -> 4.04 us
  transfers between devices with their start and end apart: 2 -> 2, of which waited for: 2 -> 0; matrix products, arithmetic and copies ran while one was open for 0% -> 1% of each run, Pallas kernels for 0% -> 48%
where the time goes in v2:
time: 151 us; the launch traced here: 153 us
  Pallas kernels  114 us (75%)
  loops' own time  15.9 us (11%)
  other arithmetic  8.31 us (6%)
  starting transfers between devices  7.42 us (5%)
  local copies, waits for them, and re-layouts  4.81 us (3%)
  between operations  2.39 us (2%)
    pallas_call x1, Pallas kernels, gather_relations(): pl.pallas_call(functools.partial(gather_kernel, bits), out_shape=jax.Shap...  45.1 us
    pallas_call x1, Pallas kernels, train_bucket(): pl.pallas_call(bucket_kernel, out_shape=(jax.ShapeDtypeStruct((rows, widt...  40.8 us
    pallas_call x1, Pallas kernels, sum_relations(): pl.pallas_call(functools.partial(sum_kernel, bits), out_shape=jax.ShapeDt...  28.6 us
    unnamed x1, loops' own time  15.2 us
    ppermute x2, starting transfers between devices, with_mask(): return lambda v, x: (lax.ppermute(v, axis, pairs), beside(x, size))  7.42 us
    unnamed x14, local copies, waits for them, and re-layouts  4.04 us
  transfers between devices with their start and end apart: 2, of which 0 were waited for; matrix products, arithmetic and copies ran while one was open for 1% of the time, Pallas kernels for 48%

profile of v2, /device:TPU:0, one launch (start us, length us, event | category | flops | bytes accessed | tf_op | source)
XLA Modules:
  0.0 153.2 jit_solution(7211711947629088706)
XLA Ops:
  1.9 1.0 fusion.10
  3.0 0.8 reshape.96.negs_ref
  3.8 0.9 convert_element_type.74
  4.7 1.5 copy.16.own_ref
  6.2 0.1 convert_element_type.73
  6.2 0.0 copy-start
  6.2 0.0 copy-start.1
  6.3 50.9 %conditional.4 = (bf16[512,400]{1,0:T(8,128)(2,1)}, bf16[2048,400]{1,0:T(8,128)(2,1)S(1)}) conditional(s32[]{:T(128)} %bitcast.31, (bf16[512,400]{1,0:T(8,128)(2,1)S(1)}, bf16[64,400]{1,0:T(8,128)(2,1)S(1)}) %tuple.444, (bf16[512,400]{1,0:T(8,128)(2,1)S(1)}, bf16[64,400]{1,0:T(8,128)(2,1)S(1)}) %tuple.444, ...), branch_computations={%region_0.1_spmd, %region_1.2_spmd, %region_2.3_spmd, %region_3.4_... | conditional | bytes 54067256 | solution.py:279
  6.3 5.1 %collective-permute-start.23 = (bf16[512,400]{1,0:T(8,128)(2,1)S(1)}, bf16[512,400]{1,0:T(8,128)(2,1)}, u32[]{:S(2)}, u32[]{:S(2)}) collective-permute-start(bf16[512,400]{1,0:T(8,128)(2,1)S(1)} %get-tuple-element.305), channel_id=1, source_target_pairs={{0,24},{1,25},{2,26},{3,27},{4,28},{5,29},{6,30},{7,31},{8,16},{9,... | collective-permute-start | bytes 1228808 | tf_op jit(solution)/shard_map/cond/branch_23_fun/ppermute | solution.py:277
  11.4 45.1 %gather_relations.54 = bf16[32,64,400]{2,1,0:T(8,128)(2,1)S(1)} custom-call(bf16[64,400]{1,0:T(8,128)(2,1)S(1)} %get-tuple-element.306.shard_ref), custom_call_target="tpu_custom_call" | custom-call | bytes 52428800 | tf_op jit(solution)/shard_map/cond/branch_23_fun/gather_relations/pallas_call | solution.py:204
  56.5 0.0 collective-permute-done.23
  57.1 0.0 copy-start.2
  57.1 1.3 copy-done.2
  58.5 0.0 copy-done
  58.5 0.0 copy-done.1
  58.5 40.8 %bucket.1 = (f32[512,400]{1,0:T(8,128)S(1)}, bf16[512,400]{1,0:T(8,128)(2,1)S(1)}, f32[2048,400]{1,0:T(8,128)S(1)}) custom-call(s32[1]{0:T(128)S(6)} %copy.174.count_ref, f32[512,400]{1,0:T(8,128)S(1)} %copy.16.own_ref, bf16[512,400]{1,0:T(8,128)(2,1)} %get-tuple-element.395.part_ref, bf16[2048,400]{1,0:T(8,128)(2,1)} %copy-done.2, ...), custom_call_target="tpu_custom_call" | custom-call | flops 18874368000 | bytes 8192000 | tf_op jit(solution)/shard_map/bucket/pallas_call | solution.py:117
  99.3 0.0 copy-start.5
  99.3 0.0 copy-start.3
  99.3 0.0 copy-start.4
  99.3 47.1 %conditional.6 = (f32[64,400]{1,0:T(8,128)}, f32[64]{0:T(128)S(1)}, bf16[512,400]{1,0:T(8,128)(2,1)}) conditional(s32[]{:T(128)} %bitcast.31, (f32[32,64,400]{2,1,0:T(8,128)S(1)}, bf16[512,400]{1,0:T(8,128)(2,1)S(1)}) %tuple.590, (f32[32,64,400]{2,1,0:T(8,128)S(1)}, bf16[512,400]{1,0:T(8,128)(2,1)S(1)}) %tuple.605, ...), branch_computations={%region_31.33_spmd, %region_33.35_spmd, %region_35.37_spmd, %regio... | conditional | flops 51136 | bytes 54169920
  108.4 2.3 %collective-permute-start.54 = (bf16[512,400]{1,0:T(8,128)(2,1)S(1)}, bf16[512,400]{1,0:T(8,128)(2,1)}, u32[]{:S(2)}, u32[]{:S(2)}) collective-permute-start(bf16[512,400]{1,0:T(8,128)(2,1)S(1)} %get-tuple-element.368), channel_id=1, source_target_pairs={{0,24},{1,25},{2,26},{3,27},{4,28},{5,29},{6,30},{7,31},{8,16},{9,... | collective-permute-start | bytes 1228808 | tf_op jit(solution)/shard_map/cond/branch_23_fun/ppermute | solution.py:277
  110.7 28.6 %sum_relations.54 = f32[64,400]{1,0:T(8,128)} custom-call(f32[32,64,400]{2,1,0:T(8,128)S(1)} %get-tuple-element.367.grad_ref), custom_call_target="tpu_custom_call" | custom-call | bytes 52428800 | tf_op jit(solution)/shard_map/cond/branch_23_fun/sum_relations/pallas_call | solution.py:250
  139.3 1.0 multiply_reduce_fusion.23
  140.3 0.0 collective-permute-done.54
  146.4 0.5 fusion.22
  146.9 0.0 copy-done.3
  146.9 1.6 %divide_subtract_fusion.1 = f32[64,400]{1,0:T(8,128)} fusion(f32[64,400]{1,0:T(8,128)S(1)} %copy-done.3, f32[64,400]{1,0:T(8,128)} %get-tuple-element.401, f32[64]{0:T(128)S(1)} %get-tuple-element.412), kind=kLoop, calls=%fused_computation.34 | loop fusion | flops 76800 | bytes 307456 | tf_op jit(solution)/shard_map/sub | solution.py:284
  148.6 1.3 multiply_reduce_fusion.31
  149.8 0.0 copy-done.4
  149.8 0.6 fusion.23
  150.4 1.3 divide_subtract_fusion
  151.7 1.2 copy.17
  (1 shorter events, 0.0 us)
Async XLA Ops:
  6.2 52.2 %copy-start = (s32[3072]{0:T(1024)S(1)}, s32[3072]{0:T(1024)}, u32[]{:S(2)}) copy-start(s32[3072]{0:T(1024)} %param.77) | copy-start | bytes 36868
  6.2 52.2 %copy-start.1 = (s32[3072]{0:T(1024)S(1)}, s32[3072]{0:T(1024)}, u32[]{:S(2)}) copy-start(s32[3072]{0:T(1024)} %param.79) | copy-start | bytes 36868
  6.3 50.2 %collective-permute-start.23 = (bf16[512,400]{1,0:T(8,128)(2,1)S(1)}, bf16[512,400]{1,0:T(8,128)(2,1)}, u32[]{:S(2)}, u32[]{:S(2)}) collective-permute-start(bf16[512,400]{1,0:T(8,128)(2,1)S(1)} %get-tuple-element.305), channel_id=1, source_target_pairs={{0,24},{1,25},{2,26},{3,27},{4,28},{5,29},{6,30},{7,31},{8,16},{9,... | collective-permute-start | bytes 1228808 | tf_op jit(solution)/shard_map/cond/branch_23_fun/ppermute | solution.py:277
  57.1 1.3 copy-start.2
  99.3 47.1 %copy-start.5 = (f32[64]{0:T(128)S(1)}, f32[64]{0:T(128)}, u32[]{:S(2)}) copy-start(f32[64]{0:T(128)} %param.75) | copy-start | bytes 772
  99.3 47.7 %copy-start.3 = (f32[64,400]{1,0:T(8,128)S(1)}, f32[64,400]{1,0:T(8,128)}, u32[]{:S(2)}) copy-start(f32[64,400]{1,0:T(8,128)} %param.74) | copy-start | bytes 307204
  99.3 50.6 %copy-start.4 = (f32[512]{0:T(512)S(1)}, f32[512]{0:T(512)}, u32[]{:S(2)}) copy-start(f32[512]{0:T(512)} %param.73) | copy-start | bytes 6148
  108.4 31.9 %collective-permute-start.54 = (bf16[512,400]{1,0:T(8,128)(2,1)S(1)}, bf16[512,400]{1,0:T(8,128)(2,1)}, u32[]{:S(2)}, u32[]{:S(2)}) collective-permute-start(bf16[512,400]{1,0:T(8,128)(2,1)S(1)} %get-tuple-element.368), channel_id=1, source_target_pairs={{0,24},{1,25},{2,26},{3,27},{4,28},{5,29},{6,30},{7,31},{8,16},{9,... | collective-permute-start | bytes 1228808 | tf_op jit(solution)/shard_map/cond/branch_23_fun/ppermute | solution.py:277
